TPU v7x, 32 devices: a whole 2x2x4 slice. The times are simulated.
32 devices in a mesh: grp: 4 (over z), tp: 4 (over y, x), seq: 2 (over core).
Axes of the slice: x: 2, y: 2, z: 4, core: 2. Of those that a mesh axis runs over, the one named last changes fastest.
Arguments:
- tokens: bfloat16 [4096, 4096], P(('grp', 'seq')), may hold values from -6 to 6
- base_weight: bfloat16 [4096, 1024], P(None, 'tp'), may hold values from -0.09375 to 0.09375
- adapter_a: bfloat16 [256, 16, 4096], P('grp', None, 'tp'), may hold values from -0.09375 to 0.09375
- adapter_b: bfloat16 [256, 16, 1024], P('grp', None, 'tp'), may hold values from -1.5 to 1.5
- token_tenant: int32 [4096], P(('grp', 'seq')), may hold values from 0 to 255, as said below
- tenant_lists: int32 [4, 4, 12], replicated, may hold values from -1 to 255, as said below
- cotangent: bfloat16 [4096, 1024], P(('grp', 'seq'), 'tp'), may hold values from -0.3125 to 0.3125
Outputs:
- projected: bfloat16 [4096, 1024], P(('grp', 'seq'), 'tp')
- grad_a: float32 [256, 16, 4096], P('grp', None, 'tp')
- grad_b: float32 [256, 16, 1024], P('grp', None, 'tp')
Inputs may be any that keep to these rules, and one draw needn't show every extreme that they name: `token_tenant`: every token's tenant is a live entry of its data group's list. `tenant_lists`: entry [g, o, c] is -1 (an empty slot) or a tenant owned by group o, an id from o * 64 to (o + 1) * 64 - 1; the live entries of each [g, o] come first and are distinct; at most 12 are live for each g and o, and one owner has all 12 live in every data group.
All inputs are finite; a program needn't handle non-finite values.
Results may differ from a plain program's by a relative error of at most 0.015.
Values may be sent and summed in bfloat16 or wider, within the bound.
A program may use at most 64 MiB of HBM per device.

v0:
```python
import jax
import jax.numpy as jnp
from jax import lax
from jax.sharding import PartitionSpec as P

SCALE = 2.0


def build_tiles(wanted, adapter_a, adapter_b, base_index):
    live = wanted >= 0
    local_index = jnp.where(live, wanted - base_index, 0)
    keep = live[:, :, None, None]
    send_a = jnp.where(keep, adapter_a[local_index], jnp.zeros((), adapter_a.dtype))
    send_b = jnp.where(keep, adapter_b[local_index], jnp.zeros((), adapter_b.dtype))
    return (send_a, send_b)


def body(tokens, base_weight, adapter_a, adapter_b, token_tenant, tenant_lists, cotangent):
    groups = lax.axis_size("grp")
    me = lax.axis_index("grp")
    feature_part = lax.axis_index("tp")
    owned = adapter_a.shape[0]
    rank = adapter_a.shape[1]
    width_a = adapter_a.shape[2]
    width_b = adapter_b.shape[2]
    depth = tenant_lists.shape[2]
    slots = groups * depth
    rows = tokens.shape[0]
    wanted = tenant_lists[:, me, :]
    send_a, send_b = build_tiles(wanted, adapter_a, adapter_b, me * owned)
    fetched_a, fetched_b = (
        lax.all_to_all(send_a, "grp", split_axis=0, concat_axis=0, tiled=True),
        lax.all_to_all(send_b, "grp", split_axis=0, concat_axis=0, tiled=True),
    )
    base = jnp.dot(tokens, base_weight, preferred_element_type=jnp.float32)
    listed = tenant_lists[me].reshape(slots)
    member = token_tenant[:, None] == listed[None, :]
    member_float = member.astype(jnp.float32)
    member_half = member.astype(jnp.bfloat16)
    tile_a = fetched_a.reshape(slots * rank, width_a)
    tile_b = fetched_b.reshape(slots * rank, width_b)
    x_part = lax.dynamic_slice_in_dim(tokens, feature_part * width_a, width_a, 1)
    contract = (((1,), (1,)), ((), ()))
    u_all = lax.dot_general(x_part, tile_a, contract, preferred_element_type=jnp.float32)
    g_all = lax.dot_general(cotangent, tile_b, contract, preferred_element_type=jnp.float32)
    u_part = jnp.sum(u_all.reshape(rows, slots, rank) * member_float[:, :, None], axis=1)
    g_part = jnp.sum(g_all.reshape(rows, slots, rank) * member_float[:, :, None], axis=1)
    low_sum, back_sum = (
        lax.psum(u_part.astype(jnp.bfloat16), "tp").astype(jnp.float32),
        lax.psum(g_part.astype(jnp.bfloat16), "tp").astype(jnp.float32),
    )
    low_half = low_sum.astype(jnp.bfloat16)
    back_half = (SCALE * back_sum).astype(jnp.bfloat16)
    low_wide = (member_half[:, :, None] * low_half[:, None, :]).reshape(rows, slots * rank)
    back_wide = (member_half[:, :, None] * back_half[:, None, :]).reshape(rows, slots * rank)
    delta = jnp.dot(low_wide, tile_b, preferred_element_type=jnp.float32)
    projected = (base + SCALE * delta).astype(jnp.bfloat16)
    over_rows = (((0,), (0,)), ((), ()))
    part_a = lax.dot_general(back_wide, x_part, over_rows, preferred_element_type=jnp.float32)
    part_a = part_a.astype(jnp.bfloat16).reshape(groups, depth, rank, width_a)
    part_b = SCALE * lax.dot_general(
        low_wide, cotangent, over_rows, preferred_element_type=jnp.float32
    )
    part_b = part_b.astype(jnp.bfloat16).reshape(groups, depth, rank, width_b)
    total_a, total_b = (
        lax.psum(part_a, "seq").astype(jnp.float32),
        lax.psum(part_b, "seq").astype(jnp.float32),
    )
    arrived_a, arrived_b = (
        lax.all_to_all(
            total_a.astype(jnp.bfloat16), "grp", split_axis=0, concat_axis=0, tiled=True
        ),
        lax.all_to_all(
            total_b.astype(jnp.bfloat16), "grp", split_axis=0, concat_axis=0, tiled=True
        ),
    )
    owner_hit = (
        (wanted - me * owned).reshape(slots)[None, :] == jnp.arange(owned)[:, None]
    ).astype(jnp.float32)
    grad_a = jnp.dot(
        owner_hit,
        arrived_a.reshape(slots, rank * width_a).astype(jnp.float32),
        precision=lax.Precision.HIGHEST,
        preferred_element_type=jnp.float32,
    )
    grad_b = jnp.dot(
        owner_hit,
        arrived_b.reshape(slots, rank * width_b).astype(jnp.float32),
        precision=lax.Precision.HIGHEST,
        preferred_element_type=jnp.float32,
    )
    return (projected, grad_a.reshape(owned, rank, width_a), grad_b.reshape(owned, rank, width_b))


def solution(mesh):
    return jax.shard_map(
        body,
        mesh=mesh,
        in_specs=(
            P(("grp", "seq"), None),
            P(None, "tp"),
            P("grp", None, "tp"),
            P("grp", None, "tp"),
            P(("grp", "seq")),
            P(),
            P(("grp", "seq"), "tp"),
        ),
        out_specs=(P(("grp", "seq"), "tp"), P("grp", None, "tp"), P("grp", None, "tp")),
        check_vma=False,
    )
```

profile of v0, /device:TPU:0, one launch (start us, length us, event | category | flops | bytes accessed | tf_op | source)
XLA Modules:
  0.0 185.7 jit_solution(7136454837934852158)
XLA Ops:
  7.2 0.0 copy-start
  7.2 0.9 broadcast_compare_fusion
  8.0 0.7 subtract_reduce_fusion
  8.8 0.1 reshape.169
  8.9 1.6 gather_fusion.1
  10.5 0.9 broadcast_select_fusion.1
  11.4 6.3 %all-to-all-start.1 = ((bf16[4,12,16,256]{3,2,1,0:T(8,128)(2,1)}), bf16[4,12,16,256]{3,2,1,0:T(8,128)(2,1)S(1)}, u32[]{:S(2)}, u32[]{:S(2)}) async-start(bf16[4,12,16,256]{3,2,1,0:T(8,128)(2,1)} %broadcast_select_fusion.1), calls=%async_computation.1 | async-start | bytes 786432 | tf_op jit(solution)/shard_map/all_to_all | solution.py:33
  17.7 0.0 copy-done
  17.7 1.9 gather_fusion
  19.5 2.7 %broadcast_select_fusion = bf16[4,12,16,1024]{3,2,1,0:T(8,128)(2,1)} fusion(bf16[4,12,16,1024]{3,2,1,0:T(8,128)(2,1)} %bitcast.58, pred[4,12]{1,0:T(4,128)(4,1)S(1)} %bitcast.70), kind=kLoop, calls=%fused_computation.11 | loop fusion | flops 786432 | bytes 3145776 | tf_op jit(solution)/shard_map/jit(_where)/select_n | solution.py:13
  22.3 0.0 copy-start.4
  22.3 0.0 copy-start.3
  22.3 7.1 %all-to-all-done.1 = bf16[4,12,16,256]{3,2,1,0:T(8,128)(2,1)S(1)} async-done(((bf16[4,12,16,256]{3,2,1,0:T(8,128)(2,1)}), bf16[4,12,16,256]{3,2,1,0:T(8,128)(2,1)S(1)}, u32[]{:S(2)}, u32[]{:S(2)}) %all-to-all-start.1) | async-done | bytes 393248 | tf_op jit(solution)/shard_map/all_to_all | solution.py:33
  29.4 4.3 %all-to-all-start = ((bf16[4,12,16,1024]{3,2,1,0:T(8,128)(2,1)}), bf16[4,12,16,1024]{3,2,1,0:T(8,128)(2,1)}, u32[]{:S(2)}, u32[]{:S(2)}) async-start(bf16[4,12,16,1024]{3,2,1,0:T(8,128)(2,1)} %broadcast_select_fusion), calls=%async_computation | async-start | bytes 3145728 | tf_op jit(solution)/shard_map/all_to_all | solution.py:32
  33.7 0.0 all-reduce.4.cloned.1.call-start
  33.8 0.7 constant_dynamic-slice_fusion.1
  34.5 0.1 eq.36
  34.5 0.0 copy-done.4
  34.5 0.1 compare_convert_fusion.1
  34.6 0.0 copy-done.3
  34.6 0.4 fusion.25
  35.0 0.9 fusion.3
  36.0 34.0 %all-to-all-done = bf16[4,12,16,1024]{3,2,1,0:T(8,128)(2,1)} async-done(((bf16[4,12,16,1024]{3,2,1,0:T(8,128)(2,1)}), bf16[4,12,16,1024]{3,2,1,0:T(8,128)(2,1)}, u32[]{:S(2)}, u32[]{:S(2)}) %all-to-all-start) | async-done | bytes 1572896 | tf_op jit(solution)/shard_map/all_to_all | solution.py:32
  69.9 3.1 %multiply_reduce_fusion = bf16[512,16]{0,1:T(8,128)(2,1)S(1)} fusion(bf16[48,16,1024]{2,1,0:T(8,128)(2,1)} %bitcast.3, bf16[512,4096]{1,0:T(8,128)(2,1)} %param.7, s32[]{:T(128)S(6)} %select_n.41, f32[512,48]{0,1:T(8,128)S(1)} %get-tuple-element.18), kind=kOutput, calls=%fused_computation.10 | convolution fusion | flops 806084608 | bytes 2736132 | tf_op jit(solution)/shard_map/dot_general | solution.py:44
  73.1 16.3 %all-reduce = (bf16[512,16]{0,1:T(8,128)(2,1)S(1)}, bf16[512,16]{0,1:T(8,128)(2,1)S(1)}) all-reduce(bf16[512,16]{0,1:T(8,128)(2,1)S(1)} %multiply_reduce_fusion, bf16[512,16]{0,1:T(8,128)(2,1)S(1)} %fusion.3), channel_id=1, replica_groups=mesh['grp'=4,'tp'=4,'seq'=2] {'tp'}, use_global_device_ids=true, to_apply=%region_1.2 | all-reduce | flops 16384 | bytes 65536 | tf_op jit(solution)/shard_map/psum | solution.py:49
  89.4 0.1 broadcast_multiply_fusion
  89.5 0.0 copy-start.1
  89.5 3.6 %convolution_convert_fusion = bf16[768,1024]{1,0:T(8,128)(2,1)} fusion(bf16[512,768]{0,1:T(8,128)(2,1)S(1)} %bitcast.66, bf16[512,4096]{1,0:T(8,128)(2,1)} %param.7, s32[]{:T(128)S(6)} %select_n.41), kind=kOutput, calls=%fused_computation.2 | convolution fusion | flops 806092800 | bytes 3407876 | tf_op jit(solution)/shard_map/dot_general | solution.py:59
  93.2 0.0 copy-done.1
  93.2 1.1 fusion.8
  94.3 0.0 all-reduce.4.cloned.1.call-update
  94.4 18.4 %all-reduce.4.cloned.1.call-done = (bf16[4,12,16,1024]{3,2,1,0:T(8,128)(2,1)}, bf16[4,12,16,256]{3,2,1,0:T(8,128)(2,1)}) async-done(((bf16[4,12,16,1024]{3,2,1,0:T(8,128)(2,1)}, bf16[4,12,16,256]{3,2,1,0:T(8,128)(2,1)}), (bf16[4,12,16,1024]{3,2,1,0:T(8,128)(2,1)}, bf16[4,12,16,256]{3,2,1,0:T(8,128)(2,1)})) %all-reduce.4.cloned.1.call-update) | async-done | bytes 1966096 | tf_op jit(solution)/shard_map/psum | solution.py:66
  112.8 17.0 %all_to_all.20 = bf16[4,12,16,256]{3,2,1,0:T(8,128)(2,1)S(1)} all-to-all(bf16[4,12,16,256]{3,2,1,0:T(8,128)(2,1)} %get-tuple-element.12), channel_id=1, replica_groups=mesh['grp'=4,'tp'=4,'seq'=2] {'grp'}, dimensions={0} | all-to-all | bytes 786432 | tf_op jit(solution)/shard_map/all_to_all | solution.py:73
  129.8 4.5 %all-to-all-start.2 = ((bf16[4,12,16,1024]{3,2,1,0:T(8,128)(2,1)}), bf16[4,12,16,1024]{3,2,1,0:T(8,128)(2,1)}, u32[]{:S(2)}, u32[]{:S(2)}) async-start(bf16[4,12,16,1024]{3,2,1,0:T(8,128)(2,1)} %get-tuple-element.11), calls=%async_computation.2 | async-start | bytes 3145728 | tf_op jit(solution)/shard_map/all_to_all | solution.py:70
  134.3 0.1 sub.25
  134.4 0.0 copy-start.2
  134.4 4.2 %fusion.24 = f32[512,256]{1,0:T(8,128)S(1)} fusion(bf16[512,4096]{1,0:T(8,128)(2,1)} %param.7, bf16[4096,256]{1,0:T(8,128)(2,1)} %param.8), kind=kOutput, calls=%fused_computation.45 | convolution fusion | flops 1073741824 | bytes 6815744 | tf_op jit(solution)/shard_map/dot_general | solution.py:35
  138.6 0.0 copy-done.2
  138.6 1.1 fusion.10
  139.7 0.4 fusion.14
  140.1 1.6 copy.19
  141.7 29.1 %all-to-all-done.2 = bf16[4,12,16,1024]{3,2,1,0:T(8,128)(2,1)} async-done(((bf16[4,12,16,1024]{3,2,1,0:T(8,128)(2,1)}), bf16[4,12,16,1024]{3,2,1,0:T(8,128)(2,1)}, u32[]{:S(2)}, u32[]{:S(2)}) %all-to-all-start.2) | async-done | bytes 1572896 | tf_op jit(solution)/shard_map/all_to_all | solution.py:70
  170.8 3.7 %fusion = f32[64,16,1024]{2,0,1:T(8,128)S(1)} fusion(s32[48]{0:T(128)S(1)} %sub.25, bf16[6,8,16,1024]{3,2,1,0:T(8,128)(2,1)} %bitcast.23), kind=kOutput, calls=%fused_computation.3 | convolution fusion | flops 100666368 | bytes 5767360 | tf_op jit(solution)/shard_map/dot_general | solution.py:80
  174.4 4.4 %copy.18 = f32[64,16,1024]{2,1,0:T(8,128)} copy(f32[64,16,1024]{2,0,1:T(8,128)S(1)} %fusion) | data formatting | bytes 8388608
  (4 shorter events, 0.0 us)
Async XLA Ops:
  7.2 10.5 %copy-start = (bf16[64,16,1024]{2,1,0:T(8,128)(2,1)S(1)}, bf16[64,16,1024]{2,1,0:T(8,128)(2,1)}, u32[]{:S(2)}) copy-start(bf16[64,16,1024]{2,1,0:T(8,128)(2,1)} %param.9) | copy-start | bytes 6291460
  11.4 18.0 %all-to-all-start.1 = ((bf16[4,12,16,256]{3,2,1,0:T(8,128)(2,1)}), bf16[4,12,16,256]{3,2,1,0:T(8,128)(2,1)S(1)}, u32[]{:S(2)}, u32[]{:S(2)}) async-start(bf16[4,12,16,256]{3,2,1,0:T(8,128)(2,1)} %broadcast_select_fusion.1), calls=%async_computation.1 | async-start | bytes 786432 | tf_op jit(solution)/shard_map/all_to_all | solution.py:33
  22.3 12.3 %copy-start.4 = (s32[512]{0:T(512)S(1)}, s32[512]{0:T(512)}, u32[]{:S(2)}) copy-start(s32[512]{0:T(512)} %param.11) | copy-start | bytes 6148
  22.3 12.4 %copy-start.3 = (bf16[512,256]{1,0:T(8,128)(2,1)S(1)}, bf16[512,256]{1,0:T(8,128)(2,1)}, u32[]{:S(2)}) copy-start(bf16[512,256]{1,0:T(8,128)(2,1)} %param.13) | copy-start | bytes 786436
  29.4 40.6 %all-to-all-start = ((bf16[4,12,16,1024]{3,2,1,0:T(8,128)(2,1)}), bf16[4,12,16,1024]{3,2,1,0:T(8,128)(2,1)}, u32[]{:S(2)}, u32[]{:S(2)}) async-start(bf16[4,12,16,1024]{3,2,1,0:T(8,128)(2,1)} %broadcast_select_fusion), calls=%async_computation | async-start | bytes 3145728 | tf_op jit(solution)/shard_map/all_to_all | solution.py:32
  33.7 79.0 %all-reduce.4.cloned.1.call-start = ((), (), s32[]{:S(2)}) async-start(), calls=%async_computation.4 | async-start | bytes 3932160 | tf_op jit(solution)/shard_map/psum | solution.py:66
  89.5 3.7 %copy-start.1 = (bf16[512,48,16]{0,2,1:T(8,128)(2,1)}, bf16[512,48,16]{0,2,1:T(8,128)(2,1)S(1)}, u32[]{:S(2)}) copy-start(bf16[512,48,16]{0,2,1:T(8,128)(2,1)S(1)} %get-tuple-element.14) | copy-start | bytes 2359300
  129.8 41.0 %all-to-all-start.2 = ((bf16[4,12,16,1024]{3,2,1,0:T(8,128)(2,1)}), bf16[4,12,16,1024]{3,2,1,0:T(8,128)(2,1)}, u32[]{:S(2)}, u32[]{:S(2)}) async-start(bf16[4,12,16,1024]{3,2,1,0:T(8,128)(2,1)} %get-tuple-element.11), calls=%async_computation.2 | async-start | bytes 3145728 | tf_op jit(solution)/shard_map/all_to_all | solution.py:70
  134.4 4.2 %copy-start.2 = (bf16[512,48,16]{0,2,1:T(8,128)(2,1)S(1)}, bf16[512,48,16]{0,2,1:T(8,128)(2,1)}, u32[]{:S(2)}) copy-start(bf16[512,48,16]{0,2,1:T(8,128)(2,1)} %copy-done.1) | copy-start | bytes 2359300
Sparse Core Ops, SparseCore 0:
  94.5 18.2 all-reduce.3
where the time goes:
time: 186 us
  waiting for transfers between devices  88.6 us (48%)
  blocking collectives  33.3 us (18%)
  matrix products  17.7 us (10%)
  starting transfers between devices  15.2 us (8%)
  between operations  14.2 us (8%)
  local copies, waits for them, and re-layouts  10.5 us (6%)
  other arithmetic  6.28 us (3%)
    all_to_all x1, waiting for transfers between devices, body(): lax.all_to_all(send_a, 'grp', split_axis=0, concat_axis=0, tiled=True)  34 us
    all_to_all x1, waiting for transfers between devices, body(): lax.all_to_all(total_a.astype(jnp.bfloat16), 'grp', split_axis=0, concat_...  29.1 us
    psum x1, waiting for transfers between devices, body(): lax.psum(part_a, 'seq').astype(jnp.float32)  18.4 us
    all_to_all x1, blocking collectives, body(): lax.all_to_all(total_b.astype(jnp.bfloat16), 'grp', split_axis=0, concat_...  17 us
    psum x1, blocking collectives, body(): lax.psum(u_part.astype(jnp.bfloat16), 'tp').astype(jnp.float32)  16.3 us
    all_to_all x1, waiting for transfers between devices, body(): lax.all_to_all(send_b, 'grp', split_axis=0, concat_axis=0, tiled=True)  7.09 us
    all_to_all x1, starting transfers between devices, body(): lax.all_to_all(send_b, 'grp', split_axis=0, concat_axis=0, tiled=True)  6.32 us
    unnamed x13, local copies, waits for them, and re-layouts  6.06 us
  transfers between devices with their start and end apart: 4, of which 4 were waited for; matrix products, arithmetic and copies ran while one was open for 8% of the time, Pallas kernels for 0%

commit v1 on v0

v1 whole, which is shorter than its diff:
```python
import functools

import jax
import jax.numpy as jnp
from jax import lax
from jax.experimental import pallas as pl
from jax.experimental.pallas import tpu as pltpu
from jax.sharding import PartitionSpec as P

SCALE = 2.0
MESH = pl.DeviceIdType.MESH


def visit_order(groups):
    order = [0]
    for d in range(1, groups // 2 + 1):
        for k in (d, groups - d):
            if k not in order:
                order.append(k)
    return order


def exchange_kernel(
    dims,
    lists_ref,
    tenant_ref,
    tokens_ref,
    weight_ref,
    ad_a_ref,
    ad_b_ref,
    cot_ref,
    proj_ref,
    out_ref,
    xv,
    wv,
    av,
    bv,
    cv,
    fetched,
    sendf,
    ug,
    ugr,
    wide,
    part,
    rsr,
    gsum,
    arr,
    acc,
    load_sem,
    out_sem,
    f_send,
    f_recv,
    fs_send,
    fs_recv,
    tp_send,
    tp_recv,
    rs_send,
    rs_recv,
    z_send,
    z_recv,
    zs_send,
    zs_recv,
):
    G, T, S, share, rank, owned, wa, wb, rows = dims
    R = share * rank
    full = S * R
    me = lax.axis_index("grp")
    tp = lax.axis_index("tp")
    s = lax.axis_index("seq")

    load_a = pltpu.make_async_copy(ad_a_ref, av, load_sem.at[0])
    load_b = pltpu.make_async_copy(ad_b_ref, bv, load_sem.at[1])
    load_a.start()
    load_b.start()
    load_c = pltpu.make_async_copy(cot_ref, cv, load_sem.at[2])
    load_x, load_w = [], []
    for j in range(T):
        at = pl.multiple_of(lax.rem(tp + j, T) * wa, 128)
        load_x.append(
            pltpu.make_async_copy(tokens_ref.at[:, pl.ds(at, wa)], xv.at[j], load_sem.at[3 + j])
        )
        load_w.append(
            pltpu.make_async_copy(weight_ref.at[pl.ds(at, wa), :], wv.at[j], load_sem.at[3 + T + j])
        )
    load_x[0].start()
    load_c.start()
    for j in range(T):
        if j:
            load_x[j].start()
        load_w[j].start()

    barrier = pltpu.get_barrier_semaphore()
    for k in range(1, G):
        pl.semaphore_signal(
            barrier, inc=1, device_id={"grp": lax.rem(me + k, G)}, device_id_type=MESH
        )
    for k in range(1, T):
        pl.semaphore_signal(
            barrier, inc=1, device_id={"tp": lax.rem(tp + k, T)}, device_id_type=MESH
        )
    for k in range(1, S):
        pl.semaphore_signal(
            barrier, inc=1, device_id={"seq": lax.rem(s + k, S)}, device_id_type=MESH
        )

    order = visit_order(G)
    sends = []

    def gather(dst, row, target, slot):
        at = jnp.clip(lists_ref[target, me, slot] - me * owned, 0, owned - 1)
        dst[pl.ds(row, rank), pl.ds(0, wa)] = av[at]
        dst[pl.ds(row, rank), pl.ds(wa, wb)] = bv[at]

    load_a.wait()
    load_b.wait()
    fetch = {}
    first = True
    for k in order[1:]:
        target = lax.rem(me + k, G)
        for j in range(share):
            gather(sendf.at[k - 1], j * rank, target, s * share + j)
        if first:
            pl.semaphore_wait(barrier, (G - 1) + (T - 1) + (S - 1))
            first = False
        fetch[k] = pltpu.make_async_remote_copy(
            src_ref=sendf.at[k - 1],
            dst_ref=fetched.at[k, s],
            send_sem=f_send.at[k],
            recv_sem=f_recv.at[k],
            device_id={"grp": target},
            device_id_type=MESH,
        )
        fetch[k].start()
        sends.append(fetch[k])
    if first:
        pl.semaphore_wait(barrier, (G - 1) + (T - 1) + (S - 1))
    for j in range(S * share):
        gather(fetched.at[0, j // share], (j % share) * rank, me, j)

    ids = tenant_ref[...]

    def members(k):
        owner = lax.rem(me - k + G, G)
        return [ids == lists_ref[me, owner, j] for j in range(S * share)]

    def spread(sem_s, sem_r, k, ref):
        out = []
        for q in range(1, S):
            copy = pltpu.make_async_remote_copy(
                src_ref=ref,
                dst_ref=ref,
                send_sem=sem_s.at[k, q],
                recv_sem=sem_r.at[k, q],
                device_id={"seq": lax.rem(s + q, S)},
                device_id_type=MESH,
            )
            copy.start()
            sends.append(copy)
            out.append(copy)
        return out

    fetch_spread, tp_copies, rs_copies, z_copies, z_spread = {}, {}, {}, {}, {}

    def take_fetch(k):
        fetch[k].wait_recv()
        fetch_spread[k] = spread(fs_send, fs_recv, k, fetched.at[k, s])

    def project(k):
        for copy in fetch_spread.get(k, ()):
            copy.wait_recv()
        tile = fetched[k].reshape(full, wa + wb)
        nt = (((1,), (1,)), ((), ()))
        u = lax.dot_general(tile[:, :wa], xv[0], nt, preferred_element_type=jnp.float32)
        g = lax.dot_general(tile[:, wa:], cv[...], nt, preferred_element_type=jnp.float32)
        us = jnp.zeros((rank, rows), jnp.float32)
        gs = jnp.zeros((rank, rows), jnp.float32)
        for j, m in enumerate(members(k)):
            mm = jnp.broadcast_to(m, (rank, rows))
            us = us + jnp.where(mm, u[j * rank : (j + 1) * rank], 0.0)
            gs = gs + jnp.where(mm, g[j * rank : (j + 1) * rank], 0.0)
        ug[k, pl.ds(0, rank), :] = us.astype(jnp.bfloat16)
        ug[k, pl.ds(rank, rank), :] = gs.astype(jnp.bfloat16)
        tp_copies[k] = []
        for q in range(1, T):
            copy = pltpu.make_async_remote_copy(
                src_ref=ug.at[k],
                dst_ref=ugr.at[k, q - 1],
                send_sem=tp_send.at[k, q],
                recv_sem=tp_recv.at[k, q],
                device_id={"tp": lax.rem(tp + q, T)},
                device_id_type=MESH,
            )
            copy.start()
            sends.append(copy)
            tp_copies[k].append(copy)

    def gradients(k):
        total = ug[k].astype(jnp.float32)
        for q in range(1, T):
            tp_copies[k][q - 1].wait_recv()
            total = total + ugr[k, q - 1].astype(jnp.float32)
        low = total[:rank].astype(jnp.bfloat16).astype(jnp.float32)
        back = (SCALE * total[rank:]).astype(jnp.bfloat16).astype(jnp.float32)
        mem = [jnp.broadcast_to(m, (rank, rows)) for m in members(k)]
        low_wide = jnp.concatenate(
            [jnp.where(m, low, 0.0).astype(jnp.bfloat16) for m in mem], axis=0
        )
        back_wide = jnp.concatenate(
            [jnp.where(m, back, 0.0).astype(jnp.bfloat16) for m in mem], axis=0
        )
        wide[k] = low_wide
        pa = jnp.dot(back_wide, xv[0], preferred_element_type=jnp.float32)
        pb = SCALE * jnp.dot(low_wide, cv[...], preferred_element_type=jnp.float32)
        part[k, :, :, pl.ds(0, wa)] = pa.astype(jnp.bfloat16).reshape(S, R, wa)
        part[k, :, :, pl.ds(wa, wb)] = pb.astype(jnp.bfloat16).reshape(S, R, wb)
        rs_copies[k] = []
        for q in range(1, S):
            peer = lax.rem(s + q, S)
            copy = pltpu.make_async_remote_copy(
                src_ref=part.at[k, peer],
                dst_ref=rsr.at[k, q - 1],
                send_sem=rs_send.at[k, q],
                recv_sem=rs_recv.at[k, q],
                device_id={"seq": peer},
                device_id_type=MESH,
            )
            copy.start()
            sends.append(copy)
            rs_copies[k].append(copy)

    def group_sum(k):
        total = part[k, s].astype(jnp.float32)
        for q in range(1, S):
            rs_copies[k][q - 1].wait_recv()
            total = total + rsr[k, q - 1].astype(jnp.float32)
        if k == 0:
            arr[0, s] = total.astype(jnp.bfloat16)
            z_spread[0] = spread(zs_send, zs_recv, 0, arr.at[0, s])
            return
        gsum[k - 1] = total.astype(jnp.bfloat16)
        z_copies[k] = pltpu.make_async_remote_copy(
            src_ref=gsum.at[k - 1],
            dst_ref=arr.at[k, s],
            send_sem=z_send.at[k],
            recv_sem=z_recv.at[k],
            device_id={"grp": lax.rem(me - k + G, G)},
            device_id_type=MESH,
        )
        z_copies[k].start()
        sends.append(z_copies[k])

    load_x[0].wait()
    load_c.wait()
    project(0)
    for j in range(T):
        if j:
            load_x[j].wait()
        load_w[j].wait()
        term = jnp.dot(xv[j], wv[j], preferred_element_type=jnp.float32)
        acc[...] = term if j == 0 else acc[...] + term
    gradients(0)
    group_sum(0)

    for i in range(1, G, 2):
        pair = order[i : i + 2]
        for k in pair:
            take_fetch(k)
        for k in pair:
            project(k)
        for k in pair:
            gradients(k)
        for k in pair:
            group_sum(k)

    outs = []

    def put_out(k):
        for copy in z_spread[k]:
            copy.wait_recv()
        copy = pltpu.make_async_copy(arr.at[k], out_ref.at[k], out_sem.at[k])
        copy.start()
        outs.append(copy)

    put_out(0)
    low_all = wide[...].reshape(G * full, rows)
    b_all = fetched[:, :, :, pl.ds(wa, wb)].reshape(G * full, wb)
    delta = lax.dot_general(
        low_all, b_all, (((0,), (0,)), ((), ())), preferred_element_type=jnp.float32
    )
    proj_ref[...] = (acc[...] + SCALE * delta).astype(jnp.bfloat16)

    for k in order[1:]:
        z_copies[k].wait_recv()
        z_spread[k] = spread(zs_send, zs_recv, k, arr.at[k, s])
    for k in order[1:]:
        put_out(k)
    for copy in outs:
        copy.wait()
    for copy in sends:
        copy.wait_send()


def owner_kernel(dims, lists_ref, arr_ref, proj_in, proj_ref, ga_ref, gb_ref, buf_a, buf_b, sem):
    G, T, S, share, rank, owned, wa, wb, rows = dims
    me = lax.axis_index("grp")
    slots = S * share
    proj_ref[...] = proj_in[...]
    step = wa // 4 if wa % 512 == 0 else wa
    copies = []
    pieces = [(buf_a, ga_ref, c, c, step) for c in range(0, wa, step)]
    pieces.append((buf_b, gb_ref, 0, wa, wb))
    for n, (buf, out, at, src, size) in enumerate(pieces):
        buf[:, :, pl.ds(at, size)] = jnp.zeros((owned, rank, size), jnp.float32)

        def add(i, _, buf=buf, at=at, src=src, size=size):
            k = i // slots
            c = i - k * slots
            t = lists_ref[lax.rem(me + k, G), me, c]

            @pl.when(t >= 0)
            def _():
                row = t - me * owned
                buf[row, :, pl.ds(at, size)] += arr_ref[i, :, pl.ds(src, size)].astype(jnp.float32)

            return 0

        lax.fori_loop(0, G * slots, add, 0)
        copy = pltpu.make_async_copy(
            buf.at[:, :, pl.ds(at, size)], out.at[:, :, pl.ds(at, size)], sem.at[n]
        )
        copy.start()
        copies.append(copy)
    for copy in copies:
        copy.wait()


def body(tokens, base_weight, adapter_a, adapter_b, token_tenant, tenant_lists, cotangent):
    G = lax.axis_size("grp")
    T = lax.axis_size("tp")
    S = lax.axis_size("seq")
    owned, rank, wa = adapter_a.shape
    wb = adapter_b.shape[2]
    depth = tenant_lists.shape[2]
    rows = tokens.shape[0]
    share = -(-depth // S)
    if share * S != depth:
        tenant_lists = jnp.pad(
            tenant_lists, ((0, 0), (0, 0), (0, share * S - depth)), constant_values=-1
        )
    R = share * rank
    width = wa + wb
    dims = (G, T, S, share, rank, owned, wa, wb, rows)
    bf, f32 = jnp.bfloat16, jnp.float32
    vmem = pl.BlockSpec(memory_space=pltpu.VMEM)
    smem = pl.BlockSpec(memory_space=pltpu.SMEM)
    hbm = pl.BlockSpec(memory_space=pl.ANY)
    dma = pltpu.SemaphoreType.DMA
    proj, arrived = pl.pallas_call(
        functools.partial(exchange_kernel, dims),
        out_shape=(
            jax.ShapeDtypeStruct((rows, wb), bf),
            jax.ShapeDtypeStruct((G, S, R, width), bf),
        ),
        in_specs=[smem, vmem, hbm, hbm, hbm, hbm, hbm],
        out_specs=(vmem, hbm),
        scratch_shapes=[
            pltpu.VMEM((T, rows, wa), bf),
            pltpu.VMEM((T, wa, wb), bf),
            pltpu.VMEM((owned, rank, wa), bf),
            pltpu.VMEM((owned, rank, wb), bf),
            pltpu.VMEM((rows, wb), bf),
            pltpu.VMEM((G, S, R, width), bf),
            pltpu.VMEM((G - 1, R, width), bf),
            pltpu.VMEM((G, 2 * rank, rows), bf),
            pltpu.VMEM((G, T - 1, 2 * rank, rows), bf),
            pltpu.VMEM((G, S * R, rows), bf),
            pltpu.VMEM((G, S, R, width), bf),
            pltpu.VMEM((G, S - 1, R, width), bf),
            pltpu.VMEM((G - 1, R, width), bf),
            pltpu.VMEM((G, S, R, width), bf),
            pltpu.VMEM((rows, wb), f32),
            dma((3 + 2 * T,)),
            dma((G,)),
            dma((G,)),
            dma((G,)),
            dma((G, S)),
            dma((G, S)),
            dma((G, T)),
            dma((G, T)),
            dma((G, S)),
            dma((G, S)),
            dma((G,)),
            dma((G,)),
            dma((G, S)),
            dma((G, S)),
        ],
        compiler_params=pltpu.CompilerParams(
            collective_id=0, has_side_effects=True, vmem_limit_bytes=50 * 2**20
        ),
        name="exchange",
    )(
        tenant_lists,
        token_tenant.reshape(1, rows),
        tokens,
        base_weight,
        adapter_a,
        adapter_b,
        cotangent,
    )
    return pl.pallas_call(
        functools.partial(owner_kernel, dims),
        out_shape=(
            jax.ShapeDtypeStruct((rows, wb), bf),
            jax.ShapeDtypeStruct((owned, rank, wa), f32),
            jax.ShapeDtypeStruct((owned, rank, wb), f32),
        ),
        in_specs=[smem, vmem, vmem],
        out_specs=(vmem, hbm, hbm),
        scratch_shapes=[
            pltpu.VMEM((owned, rank, wa), f32),
            pltpu.VMEM((owned, rank, wb), f32),
            dma((5,)),
        ],
        compiler_params=pltpu.CompilerParams(vmem_limit_bytes=40 * 2**20),
        name="owner_sums",
    )(tenant_lists, arrived.reshape(G * S * share, rank, width), proj)


def solution(mesh):
    return jax.shard_map(
        body,
        mesh=mesh,
        in_specs=(
            P(("grp", "seq"), None),
            P(None, "tp"),
            P("grp", None, "tp"),
            P("grp", None, "tp"),
            P(("grp", "seq")),
            P(),
            P(("grp", "seq"), "tp"),
        ),
        out_specs=(P(("grp", "seq"), "tp"), P("grp", None, "tp"), P("grp", None, "tp")),
        check_vma=False,
    )
```

time: 186 us -> 71.6 us (0.38)
  the two profiles are of different devices: /device:TPU:0 before, /device:TPU:1 now
where the time goes in v1:
time: 71.6 us; the launch traced here: 71.3 us
  Pallas kernels  67.3 us (94%)
  local copies, waits for them, and re-layouts  3.36 us (5%)
    pallas_call x1, Pallas kernels, body(): pl.pallas_call(functools.partial(exchange_kernel, dims), out_shape=(jax.S...  57.4 us
    pallas_call x1, Pallas kernels, body(): pl.pallas_call(functools.partial(owner_kernel, dims), out_shape=(jax.Shap...  9.92 us
    unnamed x8, local copies, waits for them, and re-layouts  3.36 us

profile of v1, /device:TPU:1, one launch (start us, length us, event | category | flops | bytes accessed | tf_op | source)
XLA Modules:
  0.0 71.3 jit_solution(7976757313469788415)
XLA Ops:
  0.6 0.0 copy-start
  0.6 1.0 %copy-done = bf16[64,16,256]{2,1,0:T(8,128)(2,1)S(1)} copy-done((bf16[64,16,256]{2,1,0:T(8,128)(2,1)S(1)}, bf16[64,16,256]{2,1,0:T(8,128)(2,1)}, u32[]{:S(2)}) %copy-start) | copy-done | bytes 524312
  1.7 0.0 copy-start.1
  1.7 0.9 %copy-done.1 = bf16[512,256]{1,0:T(8,128)(2,1)S(1)} copy-done((bf16[512,256]{1,0:T(8,128)(2,1)S(1)}, bf16[512,256]{1,0:T(8,128)(2,1)}, u32[]{:S(2)}) %copy-start.1) | copy-done | bytes 262168
  2.6 0.0 copy-start.2
  2.6 0.7 copy-done.2
  3.3 0.0 copy-start.3
  3.3 0.7 copy-done.3
  4.0 57.4 %exchange.1 = (bf16[512,256]{1,0:T(8,128)(2,1)S(1)}, bf16[4,2,96,1280]{3,2,1,0:T(8,128)(2,1)S(1)}) custom-call(s32[4,4,12]{2,1,0:T(4,128)S(1)} %copy-done.2, s32[1,512]{1,0:T(1,128)S(1)} %bitcast.3, bf16[512,4096]{1,0:T(8,128)(2,1)} %tokens_ref.1, bf16[4096,256]{1,0:T(8,128)(2,1)} %weight_ref.1, bf16[64,16,1024]{2,1,0:T(8,128)(2,1)} %ad_a_ref.1, ...), custom_call_target="tpu_custom_call" | custom-call | tf_op jit(solution)/shard_map/exchange/pallas_call | solution.py:358
  61.4 9.9 %owner_sums.1 = (bf16[512,256]{1,0:T(8,128)(2,1)}, f32[64,16,1024]{2,1,0:T(8,128)}, f32[64,16,256]{2,1,0:T(8,128)}) custom-call(s32[4,4,12]{2,1,0:T(4,128)S(1)} %copy-done.2, bf16[48,16,1280]{2,1,0:T(8,128)(2,1)S(1)} %bitcast.2, bf16[512,256]{1,0:T(8,128)(2,1)S(1)} %get-tuple-element.6.proj_in), custom_call_target="tpu_custom_call" | custom-call | tf_op jit(solution)/shard_map/owner_sums/pallas_call | solution.py:410
Async XLA Ops:
  0.6 1.0 %copy-start = (bf16[64,16,256]{2,1,0:T(8,128)(2,1)S(1)}, bf16[64,16,256]{2,1,0:T(8,128)(2,1)}, u32[]{:S(2)}) copy-start(bf16[64,16,256]{2,1,0:T(8,128)(2,1)} %ad_b_ref.1) | copy-start | bytes 1572868
  1.7 0.9 %copy-start.1 = (bf16[512,256]{1,0:T(8,128)(2,1)S(1)}, bf16[512,256]{1,0:T(8,128)(2,1)}, u32[]{:S(2)}) copy-start(bf16[512,256]{1,0:T(8,128)(2,1)} %cot_ref.1) | copy-start | bytes 786436
  2.6 0.7 copy-start.2
  3.3 0.7 copy-start.3

commit v2 on v1

--- a/solution.py
+++ b/solution.py
@@ -11,19 +11,30 @@
 MESH = pl.DeviceIdType.MESH
 
 
-def visit_order(groups):
-    order = [0]
-    for d in range(1, groups // 2 + 1):
-        for k in (d, groups - d):
-            if k not in order:
-                order.append(k)
-    return order
+def stages(groups):
+    half = groups // 2
+    if groups < 2:
+        return []
+    first = [half] + list(range(1, half))
+    return [ks for ks in (first, list(range(half + 1, groups))) if ks]
+
+
+def partners(me, k, groups):
+    if groups & (groups - 1):
+        return lax.rem(me + k, groups), lax.rem(me - k + groups, groups)
+    other = me
+    bit = 1
+    while bit < groups:
+        if k & bit:
+            other = other + bit * (1 - 2 * lax.rem(lax.div(me, bit), 2))
+        bit *= 2
+    return other, other
 
 
 def exchange_kernel(
     dims,
-    lists_ref,
-    tenant_ref,
+    lists_hbm,
+    tenant_hbm,
     tokens_ref,
     weight_ref,
     ad_a_ref,
@@ -31,6 +42,8 @@
     cot_ref,
     proj_ref,
     out_ref,
+    lists_ref,
+    tenant_ref,
     xv,
     wv,
     av,
@@ -68,10 +81,14 @@
     tp = lax.axis_index("tp")
     s = lax.axis_index("seq")
 
+    load_l = pltpu.make_async_copy(lists_hbm, lists_ref, load_sem.at[3 + 2 * T])
+    load_t = pltpu.make_async_copy(tenant_hbm, tenant_ref, load_sem.at[4 + 2 * T])
+    load_l.start()
     load_a = pltpu.make_async_copy(ad_a_ref, av, load_sem.at[0])
     load_b = pltpu.make_async_copy(ad_b_ref, bv, load_sem.at[1])
     load_a.start()
     load_b.start()
+    load_t.start()
     load_c = pltpu.make_async_copy(cot_ref, cv, load_sem.at[2])
     load_x, load_w = [], []
     for j in range(T):
@@ -103,7 +120,9 @@
             barrier, inc=1, device_id={"seq": lax.rem(s + k, S)}, device_id_type=MESH
         )
 
-    order = visit_order(G)
+    plan = stages(G)
+    order = [0] + [k for ks in plan for k in ks]
+    late = [k for ks in plan[1:] for k in ks]
     sends = []
 
     def gather(dst, row, target, slot):
@@ -111,12 +130,13 @@
         dst[pl.ds(row, rank), pl.ds(0, wa)] = av[at]
         dst[pl.ds(row, rank), pl.ds(wa, wb)] = bv[at]
 
+    load_l.wait()
     load_a.wait()
     load_b.wait()
     fetch = {}
     first = True
     for k in order[1:]:
-        target = lax.rem(me + k, G)
+        target, _ = partners(me, k, G)
         for j in range(share):
             gather(sendf.at[k - 1], j * rank, target, s * share + j)
         if first:
@@ -130,17 +150,18 @@
             device_id={"grp": target},
             device_id_type=MESH,
         )
-        fetch[k].start()
-        sends.append(fetch[k])
+        if k not in late:
+            fetch[k].start()
     if first:
         pl.semaphore_wait(barrier, (G - 1) + (T - 1) + (S - 1))
     for j in range(S * share):
         gather(fetched.at[0, j // share], (j % share) * rank, me, j)
 
+    load_t.wait()
     ids = tenant_ref[...]
 
     def members(k):
-        owner = lax.rem(me - k + G, G)
+        _, owner = partners(me, k, G)
         return [ids == lists_ref[me, owner, j] for j in range(S * share)]
 
     def spread(sem_s, sem_r, k, ref):
@@ -243,7 +264,7 @@
             dst_ref=arr.at[k, s],
             send_sem=z_send.at[k],
             recv_sem=z_recv.at[k],
-            device_id={"grp": lax.rem(me - k + G, G)},
+            device_id={"grp": partners(me, k, G)[1]},
             device_id_type=MESH,
         )
         z_copies[k].start()
@@ -261,15 +282,19 @@
     gradients(0)
     group_sum(0)
 
-    for i in range(1, G, 2):
-        pair = order[i : i + 2]
-        for k in pair:
+    for n, ks in enumerate(plan):
+        if n == 0:
+            fetch[ks[0]].wait_send()
+            for k in late:
+                fetch[k].start()
+            sends.extend(fetch[k] for k in order[1:] if k != ks[0])
+        for k in ks:
             take_fetch(k)
-        for k in pair:
+        for k in ks:
             project(k)
-        for k in pair:
+        for k in ks:
             gradients(k)
-        for k in pair:
+        for k in ks:
             group_sum(k)
 
     outs = []
@@ -300,33 +325,48 @@
         copy.wait_send()
 
 
-def owner_kernel(dims, lists_ref, arr_ref, proj_in, proj_ref, ga_ref, gb_ref, buf_a, buf_b, sem):
+def owner_kernel(
+    dims,
+    lists_hbm,
+    arr_hbm,
+    proj_in,
+    proj_ref,
+    ga_ref,
+    gb_ref,
+    lists_ref,
+    arr_ref,
+    buf_a,
+    buf_b,
+    sem,
+    load_sem,
+):
     G, T, S, share, rank, owned, wa, wb, rows = dims
     me = lax.axis_index("grp")
     slots = S * share
-    proj_ref[...] = proj_in[...]
-    step = wa // 4 if wa % 512 == 0 else wa
-    copies = []
+    load_l = pltpu.make_async_copy(lists_hbm, lists_ref, load_sem.at[0])
+    load_l.start()
+    load_arr = pltpu.make_async_copy(arr_hbm, arr_ref, load_sem.at[1])
+    load_arr.start()
+    copies = [pltpu.make_async_copy(proj_in, proj_ref, load_sem.at[2])]
+    copies[0].start()
+    step = wa // 2 if wa % 256 == 0 else wa
     pieces = [(buf_a, ga_ref, c, c, step) for c in range(0, wa, step)]
     pieces.append((buf_b, gb_ref, 0, wa, wb))
+    buf_a[...] = jnp.zeros_like(buf_a)
+    buf_b[...] = jnp.zeros_like(buf_b)
+    load_l.wait()
+    targets = []
+    for k in range(G):
+        group, _ = partners(me, k, G)
+        for c in range(slots):
+            t = lists_ref[group, me, c]
+            targets.append(jnp.where(t >= 0, t - me * owned, owned))
+    load_arr.wait()
     for n, (buf, out, at, src, size) in enumerate(pieces):
-        buf[:, :, pl.ds(at, size)] = jnp.zeros((owned, rank, size), jnp.float32)
-
-        def add(i, _, buf=buf, at=at, src=src, size=size):
-            k = i // slots
-            c = i - k * slots
-            t = lists_ref[lax.rem(me + k, G), me, c]
-
-            @pl.when(t >= 0)
-            def _():
-                row = t - me * owned
-                buf[row, :, pl.ds(at, size)] += arr_ref[i, :, pl.ds(src, size)].astype(jnp.float32)
-
-            return 0
-
-        lax.fori_loop(0, G * slots, add, 0)
+        for i, row in enumerate(targets):
+            buf[row, :, at : at + size] += arr_ref[i, :, src : src + size].astype(jnp.float32)
         copy = pltpu.make_async_copy(
-            buf.at[:, :, pl.ds(at, size)], out.at[:, :, pl.ds(at, size)], sem.at[n]
+            buf.at[pl.ds(0, owned), :, pl.ds(at, size)], out.at[:, :, pl.ds(at, size)], sem.at[n]
         )
         copy.start()
         copies.append(copy)
@@ -349,10 +389,10 @@
         )
     R = share * rank
     width = wa + wb
+    slots = share * S
     dims = (G, T, S, share, rank, owned, wa, wb, rows)
     bf, f32 = jnp.bfloat16, jnp.float32
     vmem = pl.BlockSpec(memory_space=pltpu.VMEM)
-    smem = pl.BlockSpec(memory_space=pltpu.SMEM)
     hbm = pl.BlockSpec(memory_space=pl.ANY)
     dma = pltpu.SemaphoreType.DMA
     proj, arrived = pl.pallas_call(
@@ -361,9 +401,11 @@
             jax.ShapeDtypeStruct((rows, wb), bf),
             jax.ShapeDtypeStruct((G, S, R, width), bf),
         ),
-        in_specs=[smem, vmem, hbm, hbm, hbm, hbm, hbm],
+        in_specs=[hbm] * 7,
         out_specs=(vmem, hbm),
         scratch_shapes=[
+            pltpu.SMEM((G, G, share * S), jnp.int32),
+            pltpu.VMEM((1, rows), jnp.int32),
             pltpu.VMEM((T, rows, wa), bf),
             pltpu.VMEM((T, wa, wb), bf),
             pltpu.VMEM((owned, rank, wa), bf),
@@ -379,7 +421,7 @@
             pltpu.VMEM((G - 1, R, width), bf),
             pltpu.VMEM((G, S, R, width), bf),
             pltpu.VMEM((rows, wb), f32),
-            dma((3 + 2 * T,)),
+            dma((5 + 2 * T,)),
             dma((G,)),
             dma((G,)),
             dma((G,)),
@@ -395,7 +437,7 @@
             dma((G, S)),
         ],
         compiler_params=pltpu.CompilerParams(
-            collective_id=0, has_side_effects=True, vmem_limit_bytes=50 * 2**20
+            collective_id=0, has_side_effects=True, vmem_limit_bytes=64 * 2**20
         ),
         name="exchange",
     )(
@@ -414,14 +456,17 @@
             jax.ShapeDtypeStruct((owned, rank, wa), f32),
             jax.ShapeDtypeStruct((owned, rank, wb), f32),
         ),
-        in_specs=[smem, vmem, vmem],
-        out_specs=(vmem, hbm, hbm),
+        in_specs=[hbm, hbm, hbm],
+        out_specs=(hbm, hbm, hbm),
         scratch_shapes=[
-            pltpu.VMEM((owned, rank, wa), f32),
-            pltpu.VMEM((owned, rank, wb), f32),
-            dma((5,)),
+            pltpu.SMEM((G, G, slots), jnp.int32),
+            pltpu.VMEM((G * slots, rank, width), bf),
+            pltpu.VMEM((owned + 1, rank, wa), f32),
+            pltpu.VMEM((owned + 1, rank, wb), f32),
+            dma((3,)),
+            dma((3,)),
         ],
-        compiler_params=pltpu.CompilerParams(vmem_limit_bytes=40 * 2**20),
+        compiler_params=pltpu.CompilerParams(vmem_limit_bytes=64 * 2**20),
         name="owner_sums",
     )(tenant_lists, arrived.reshape(G * S * share, rank, width), proj)
 

time: 71.6 us -> 61.5 us (0.86)
  the two profiles are of different devices: /device:TPU:1 before, /device:TPU:9 now
where the time goes in v2:
time: 61.5 us; the launch traced here: 61.3 us
  Pallas kernels  60.6 us (99%)
  between operations  0.64 us (1%)
    pallas_call x1, Pallas kernels, body(): pl.pallas_call(functools.partial(exchange_kernel, dims), out_shape=(jax.S...  51.5 us
    pallas_call x1, Pallas kernels, body(): pl.pallas_call(functools.partial(owner_kernel, dims), out_shape=(jax.Shap...  9.11 us

profile of v2, /device:TPU:9, one launch (start us, length us, event | category | flops | bytes accessed | tf_op | source)
XLA Modules:
  0.0 61.3 jit_solution(543898639752010588)
XLA Ops:
  0.6 51.5 %exchange.1 = (bf16[512,256]{1,0:T(8,128)(2,1)}, bf16[4,2,96,1280]{3,2,1,0:T(8,128)(2,1)}) custom-call(s32[4,4,12]{2,1,0:T(4,128)} %lists_hbm.3, s32[1,512]{1,0:T(1,128)} %bitcast.3, bf16[512,4096]{1,0:T(8,128)(2,1)} %tokens_ref.1, bf16[4096,256]{1,0:T(8,128)(2,1)} %weight_ref.1, bf16[64,16,1024]{2,1,0:T(8,128)(2,1)} %ad_a_ref.1, ...), custom_call_target="tpu_custom_call" | custom-call | tf_op jit(solution)/shard_map/exchange/pallas_call | solution.py:398
  52.2 9.1 %owner_sums.1 = (bf16[512,256]{1,0:T(8,128)(2,1)}, f32[64,16,1024]{2,1,0:T(8,128)}, f32[64,16,256]{2,1,0:T(8,128)}) custom-call(s32[4,4,12]{2,1,0:T(4,128)} %lists_hbm.3, bf16[48,16,1280]{2,1,0:T(8,128)(2,1)} %bitcast.2, bf16[512,256]{1,0:T(8,128)(2,1)} %get-tuple-element.6.proj_in), custom_call_target="tpu_custom_call" | custom-call | tf_op jit(solution)/shard_map/owner_sums/pallas_call | solution.py:452

commit v3 on v2

--- a/solution.py
+++ b/solution.py
@@ -164,14 +164,14 @@
         _, owner = partners(me, k, G)
         return [ids == lists_ref[me, owner, j] for j in range(S * share)]
 
-    def spread(sem_s, sem_r, k, ref):
+    def spread(sem_s, sem_r, k, ref, h=0):
         out = []
         for q in range(1, S):
             copy = pltpu.make_async_remote_copy(
                 src_ref=ref,
                 dst_ref=ref,
-                send_sem=sem_s.at[k, q],
-                recv_sem=sem_r.at[k, q],
+                send_sem=sem_s.at[k, q, h],
+                recv_sem=sem_r.at[k, q, h],
                 device_id={"seq": lax.rem(s + q, S)},
                 device_id_type=MESH,
             )
@@ -179,6 +179,11 @@
             sends.append(copy)
             out.append(copy)
         return out
+
+    def halves(k):
+        if k in late and R % 32 == 0:
+            return [(0, pl.ds(0, R // 2)), (1, pl.ds(R // 2, R // 2))]
+        return [(0, pl.ds(0, R))]
 
     fetch_spread, tp_copies, rs_copies, z_copies, z_spread = {}, {}, {}, {}, {}
 
@@ -259,16 +264,19 @@
             z_spread[0] = spread(zs_send, zs_recv, 0, arr.at[0, s])
             return
         gsum[k - 1] = total.astype(jnp.bfloat16)
-        z_copies[k] = pltpu.make_async_remote_copy(
-            src_ref=gsum.at[k - 1],
-            dst_ref=arr.at[k, s],
-            send_sem=z_send.at[k],
-            recv_sem=z_recv.at[k],
-            device_id={"grp": partners(me, k, G)[1]},
-            device_id_type=MESH,
-        )
-        z_copies[k].start()
-        sends.append(z_copies[k])
+        z_copies[k] = []
+        for h, span in halves(k):
+            copy = pltpu.make_async_remote_copy(
+                src_ref=gsum.at[k - 1, span],
+                dst_ref=arr.at[k, s, span],
+                send_sem=z_send.at[k, h],
+                recv_sem=z_recv.at[k, h],
+                device_id={"grp": partners(me, k, G)[1]},
+                device_id_type=MESH,
+            )
+            copy.start()
+            sends.append(copy)
+            z_copies[k].append(copy)
 
     load_x[0].wait()
     load_c.wait()
@@ -315,9 +323,13 @@
     proj_ref[...] = (acc[...] + SCALE * delta).astype(jnp.bfloat16)
 
     for k in order[1:]:
-        z_copies[k].wait_recv()
-        z_spread[k] = spread(zs_send, zs_recv, k, arr.at[k, s])
-    for k in order[1:]:
+        z_spread[k] = []
+        for h, span in halves(k):
+            z_copies[k][h].wait_recv()
+            z_spread[k] += spread(zs_send, zs_recv, k, arr.at[k, s, span], h)
+        if k not in late:
+            put_out(k)
+    for k in late:
         put_out(k)
     for copy in outs:
         copy.wait()
@@ -337,6 +349,7 @@
     arr_ref,
     buf_a,
     buf_b,
+    proj_v,
     sem,
     load_sem,
 ):
@@ -347,11 +360,8 @@
     load_l.start()
     load_arr = pltpu.make_async_copy(arr_hbm, arr_ref, load_sem.at[1])
     load_arr.start()
-    copies = [pltpu.make_async_copy(proj_in, proj_ref, load_sem.at[2])]
-    copies[0].start()
-    step = wa // 2 if wa % 256 == 0 else wa
-    pieces = [(buf_a, ga_ref, c, c, step) for c in range(0, wa, step)]
-    pieces.append((buf_b, gb_ref, 0, wa, wb))
+    load_p = pltpu.make_async_copy(proj_in, proj_v, load_sem.at[2])
+    load_p.start()
     buf_a[...] = jnp.zeros_like(buf_a)
     buf_b[...] = jnp.zeros_like(buf_b)
     load_l.wait()
@@ -361,15 +371,16 @@
         for c in range(slots):
             t = lists_ref[group, me, c]
             targets.append(jnp.where(t >= 0, t - me * owned, owned))
+    load_p.wait()
+    copies = [pltpu.make_async_copy(proj_v, proj_ref, sem.at[0])]
+    copies[0].start()
     load_arr.wait()
-    for n, (buf, out, at, src, size) in enumerate(pieces):
-        for i, row in enumerate(targets):
-            buf[row, :, at : at + size] += arr_ref[i, :, src : src + size].astype(jnp.float32)
-        copy = pltpu.make_async_copy(
-            buf.at[pl.ds(0, owned), :, pl.ds(at, size)], out.at[:, :, pl.ds(at, size)], sem.at[n]
-        )
-        copy.start()
-        copies.append(copy)
+    for i, row in enumerate(targets):
+        buf_a[row] += arr_ref[i, :, :wa].astype(jnp.float32)
+        buf_b[row] += arr_ref[i, :, wa:].astype(jnp.float32)
+    for n, (buf, out) in enumerate(((buf_a, ga_ref), (buf_b, gb_ref))):
+        copies.append(pltpu.make_async_copy(buf.at[pl.ds(0, owned)], out, sem.at[n + 1]))
+        copies[-1].start()
     for copy in copies:
         copy.wait()
 
@@ -425,16 +436,16 @@
             dma((G,)),
             dma((G,)),
             dma((G,)),
-            dma((G, S)),
-            dma((G, S)),
+            dma((G, S, 1)),
+            dma((G, S, 1)),
             dma((G, T)),
             dma((G, T)),
             dma((G, S)),
             dma((G, S)),
-            dma((G,)),
-            dma((G,)),
-            dma((G, S)),
-            dma((G, S)),
+            dma((G, 2)),
+            dma((G, 2)),
+            dma((G, S, 2)),
+            dma((G, S, 2)),
         ],
         compiler_params=pltpu.CompilerParams(
             collective_id=0, has_side_effects=True, vmem_limit_bytes=64 * 2**20
@@ -463,6 +474,7 @@
             pltpu.VMEM((G * slots, rank, width), bf),
             pltpu.VMEM((owned + 1, rank, wa), f32),
             pltpu.VMEM((owned + 1, rank, wb), f32),
+            pltpu.VMEM((rows, wb), bf),
             dma((3,)),
             dma((3,)),
         ],

time: 61.5 us -> 56.8 us (0.924)
  Pallas kernels: 60.6 us -> 55.9 us
    pallas_call x1, Pallas kernels: 9.11 us -> 4.34 us  [body(): pl.pallas_call(functools.partial(owner_kernel, dims), out_shape=(jax.Shap...]
where the time goes in v3:
time: 56.8 us; the launch traced here: 56.5 us
  Pallas kernels  55.9 us (98%)
  between operations  0.64 us (1%)
    pallas_call x1, Pallas kernels, body(): pl.pallas_call(functools.partial(exchange_kernel, dims), out_shape=(jax.S...  51.6 us
    pallas_call x1, Pallas kernels, body(): pl.pallas_call(functools.partial(owner_kernel, dims), out_shape=(jax.Shap...  4.34 us

profile of v3, /device:TPU:9, one launch (start us, length us, event | category | flops | bytes accessed | tf_op | source)
XLA Modules:
  0.0 56.5 jit_solution(13030251370734655571)
XLA Ops:
  0.6 51.6 %exchange.1 = (bf16[512,256]{1,0:T(8,128)(2,1)}, bf16[4,2,96,1280]{3,2,1,0:T(8,128)(2,1)}) custom-call(s32[4,4,12]{2,1,0:T(4,128)} %lists_hbm.3, s32[1,512]{1,0:T(1,128)} %bitcast.3, bf16[512,4096]{1,0:T(8,128)(2,1)} %tokens_ref.1, bf16[4096,256]{1,0:T(8,128)(2,1)} %weight_ref.1, bf16[64,16,1024]{2,1,0:T(8,128)(2,1)} %ad_a_ref.1, ...), custom_call_target="tpu_custom_call" | custom-call | tf_op jit(solution)/shard_map/exchange/pallas_call | solution.py:409
  52.2 4.3 %owner_sums.1 = (bf16[512,256]{1,0:T(8,128)(2,1)}, f32[64,16,1024]{2,1,0:T(8,128)}, f32[64,16,256]{2,1,0:T(8,128)}) custom-call(s32[4,4,12]{2,1,0:T(4,128)} %lists_hbm.3, bf16[48,16,1280]{2,1,0:T(8,128)(2,1)} %bitcast.2, bf16[512,256]{1,0:T(8,128)(2,1)} %get-tuple-element.6.proj_in), custom_call_target="tpu_custom_call" | custom-call | tf_op jit(solution)/shard_map/owner_sums/pallas_call | solution.py:463

commit v4 on v3

--- a/solution.py
+++ b/solution.py
@@ -281,12 +281,6 @@
     load_x[0].wait()
     load_c.wait()
     project(0)
-    for j in range(T):
-        if j:
-            load_x[j].wait()
-        load_w[j].wait()
-        term = jnp.dot(xv[j], wv[j], preferred_element_type=jnp.float32)
-        acc[...] = term if j == 0 else acc[...] + term
     gradients(0)
     group_sum(0)
 
@@ -315,6 +309,12 @@
         outs.append(copy)
 
     put_out(0)
+    for j in range(T):
+        if j:
+            load_x[j].wait()
+        load_w[j].wait()
+        term = jnp.dot(xv[j], wv[j], preferred_element_type=jnp.float32)
+        acc[...] = term if j == 0 else acc[...] + term
     low_all = wide[...].reshape(G * full, rows)
     b_all = fetched[:, :, :, pl.ds(wa, wb)].reshape(G * full, wb)
     delta = lax.dot_general(

time: 56.8 us -> 56.5 us (level)
  no operation moved by 1% of the time
where the time goes in v4:
time: 56.5 us; the launch traced here: 56.2 us
  Pallas kernels  55.6 us (98%)
  between operations  0.64 us (1%)
    pallas_call x1, Pallas kernels, body(): pl.pallas_call(functools.partial(exchange_kernel, dims), out_shape=(jax.S...  51.2 us
    pallas_call x1, Pallas kernels, body(): pl.pallas_call(functools.partial(owner_kernel, dims), out_shape=(jax.Shap...  4.35 us

profile of v4, /device:TPU:9, one launch (start us, length us, event | category | flops | bytes accessed | tf_op | source)
XLA Modules:
  0.0 56.2 jit_solution(1836984624327688943)
XLA Ops:
  0.6 51.2 %exchange.1 = (bf16[512,256]{1,0:T(8,128)(2,1)}, bf16[4,2,96,1280]{3,2,1,0:T(8,128)(2,1)}) custom-call(s32[4,4,12]{2,1,0:T(4,128)} %lists_hbm.3, s32[1,512]{1,0:T(1,128)} %bitcast.3, bf16[512,4096]{1,0:T(8,128)(2,1)} %tokens_ref.1, bf16[4096,256]{1,0:T(8,128)(2,1)} %weight_ref.1, bf16[64,16,1024]{2,1,0:T(8,128)(2,1)} %ad_a_ref.1, ...), custom_call_target="tpu_custom_call" | custom-call | tf_op jit(solution)/shard_map/exchange/pallas_call | solution.py:409
  51.9 4.3 %owner_sums.1 = (bf16[512,256]{1,0:T(8,128)(2,1)}, f32[64,16,1024]{2,1,0:T(8,128)}, f32[64,16,256]{2,1,0:T(8,128)}) custom-call(s32[4,4,12]{2,1,0:T(4,128)} %lists_hbm.3, bf16[48,16,1280]{2,1,0:T(8,128)(2,1)} %bitcast.2, bf16[512,256]{1,0:T(8,128)(2,1)} %get-tuple-element.6.proj_in), custom_call_target="tpu_custom_call" | custom-call | tf_op jit(solution)/shard_map/owner_sums/pallas_call | solution.py:463
